TPU v7x, 768 devices: a whole 4x8x12 slice. The times are simulated.
768 devices in a mesh: grp: 6 (over z_lo, core), blk: 128 (over x, y, z_hi).
Axes of the slice: x: 4, y: 8, z: 12 (z_hi: 4, z_lo: 3; z = z_hi * 3 + z_lo), core: 2. Of those that a mesh axis runs over, the one named last changes fastest.
Arguments:
- query_hidden: bfloat16 [98304, 2048], P(('grp', 'blk')), as said below
- query_proj: bfloat16 [2048, 512], replicated, may hold values from -0.125 to 0.125
- item_embed: bfloat16 [6144, 512], P(('grp', 'blk')), may hold values from -6 to 6
- positive: int32 [98304], P(('grp', 'blk')), may hold values from 0 to 1023
- hard_ids: int32 [98304, 8], P(('grp', 'blk')), may hold values from 0 to 1023
Outputs:
- item_grad: float32 [6144, 512], P(('grp', 'blk'))
- weight_update: float32 [2048, 512], P('blk')
Inputs may be any that keep to these rules, and one draw needn't show every extreme that they name: `positive`: index of the query's positive item among the 1024 items of its group. `hard_ids`: indices among the 1024 items of the query's group; some items are named far more often than others. `query_hidden`: hidden activations.
All inputs are finite; a program needn't handle non-finite values.
Results may differ from a plain program's by a relative error of at most 0.0053.
Values may be sent and summed in bfloat16 or wider, within the bound.
A program may use at most 64 MiB of HBM per device.

v0:
```python
import jax
import jax.numpy as jnp
from jax import lax
from jax.sharding import PartitionSpec as P

EMB = 512
HID = 2048


INV_TAU = 50.0
EPSILON = 1e-06


def normalize_rows(values):
    inverse = lax.rsqrt(jnp.sum(values * values, axis=-1, keepdims=True) + EPSILON)
    return (values * inverse, inverse)


def shards(query_hidden, query_proj, item_embed, positive, hard_ids):
    query_raw = jnp.dot(query_hidden, query_proj, preferred_element_type=jnp.float32)
    query_dir, query_inv = normalize_rows(query_raw)
    query_unit = query_dir.astype(jnp.bfloat16)
    item_dir, item_inv = normalize_rows(item_embed.astype(jnp.float32))
    item_unit = item_dir.astype(jnp.bfloat16)
    group_items = lax.all_gather(item_unit, "blk", axis=0, tiled=True)
    scores = (
        lax.dot_general(
            query_unit, group_items, (((1,), (1,)), ((), ())), preferred_element_type=jnp.float32
        )
        * INV_TAU
    )
    log_total = jnp.log(jnp.sum(jnp.exp(scores), axis=1, keepdims=True))
    soft = jnp.exp(scores - log_total)
    pos_score = jnp.take_along_axis(scores, positive[:, None], axis=1)
    hard_score = jnp.take_along_axis(scores, hard_ids, axis=1)
    hard_weight = jax.nn.sigmoid(hard_score - pos_score)
    columns = lax.broadcasted_iota(jnp.int32, scores.shape, 1)
    extra = 1.0 + jnp.sum(hard_weight, axis=1, keepdims=True)
    grad_rows = soft - jnp.where(columns == positive[:, None], extra, 0.0)
    for hard_slot in range(hard_ids.shape[1]):
        grad_rows = grad_rows + jnp.where(
            columns == hard_ids[:, hard_slot : hard_slot + 1],
            hard_weight[:, hard_slot : hard_slot + 1],
            0.0,
        )
    score_grad = (grad_rows * INV_TAU).astype(jnp.bfloat16)
    query_grad = jnp.dot(score_grad, group_items, preferred_element_type=jnp.float32)
    raw_grad = (
        query_inv
        * (query_grad - query_dir * jnp.sum(query_dir * query_grad, axis=-1, keepdims=True))
    ).astype(jnp.bfloat16)
    unit_grad = lax.psum_scatter(
        lax.dot_general(
            score_grad, query_unit, (((0,), (0,)), ((), ())), preferred_element_type=jnp.float32
        ),
        "blk",
        scatter_dimension=0,
        tiled=True,
    )
    weight_part = lax.psum_scatter(
        lax.dot_general(
            query_hidden, raw_grad, (((0,), (0,)), ((), ())), preferred_element_type=jnp.float32
        ),
        "blk",
        scatter_dimension=0,
        tiled=True,
    )
    item_grad = item_inv * (
        unit_grad - item_dir * jnp.sum(item_dir * unit_grad, axis=-1, keepdims=True)
    )
    weight_sum = lax.psum(weight_part, "grp")
    square_total = lax.psum(jnp.sum(weight_sum * weight_sum), "blk")
    weight_update = weight_sum * lax.rsqrt(square_total / (HID * EMB) + EPSILON)
    return (item_grad, weight_update)


def solution(mesh):
    return jax.shard_map(
        shards,
        mesh=mesh,
        in_specs=(
            P(("grp", "blk"), None),
            P(),
            P(("grp", "blk"), None),
            P(("grp", "blk")),
            P(("grp", "blk"), None),
        ),
        out_specs=(P(("grp", "blk"), None), P("blk", None)),
        check_vma=False,
    )
```

profile of v0, /device:TPU:64, one launch (start us, length us, event | category | flops | bytes accessed | tf_op | source)
XLA Modules:
  0.0 2226.8 jit_solution(17921004089190366560)
XLA Ops:
  7.2 0.0 all-gather.2.cloned.1.call-start
  7.2 1.0 fusion.8
  8.2 1.4 fusion.4
  9.6 0.0 all-gather.2.cloned.1.call-update
  9.6 0.0 reduce-scatter.5.cloned.1.call-start
  9.6 0.7 bitcast_or_fusion
  10.3 0.1 copy.26
  10.4 0.1 reshape.65
  10.5 0.7 fusion.9
  11.2 1.6 multiply_reduce_fusion.2
  12.8 132.3 %all-gather.2.cloned.1.call-done = bf16[1024,512]{1,0:T(8,128)(2,1)} async-done(((bf16[8,512]{1,0:T(8,128)(2,1)}), bf16[1024,512]{1,0:T(8,128)(2,1)}) %all-gather.2.cloned.1.call-update) | async-done | bytes 1048592 | tf_op jit(solution)/shard_map/all_gather | solution.py:25
  145.1 1.8 exponential_reduce_fusion
  146.9 8.6 gather_fusion
  155.5 1.5 gather_fusion.1
  157.0 0.1 reshape.68
  157.2 0.8 multiply_convert_fusion
  158.1 0.7 copy-done.2
  158.8 1.9 fusion.10
  160.7 0.0 reduce-scatter.5.cloned.1.call-update
  160.7 0.0 reduce-scatter.7.cloned.1.call-start
  160.8 1.4 multiply_reduce_fusion.1
  162.2 2.8 convolution_bitcast_fusion
  165.0 5.3 copy.29
  170.3 805.5 %reduce-scatter.5.cloned.1.call-done = f32[8,512]{1,0:T(8,128)} async-done(((f32[1024,512]{1,0:T(8,128)}), f32[8,512]{1,0:T(8,128)}) %reduce-scatter.5.cloned.1.call-update) | async-done | bytes 16400 | tf_op jit(solution)/shard_map/reduce_scatter | solution.py:52
  975.8 0.9 fusion.5
  976.7 816.8 %reduce-scatter.7.cloned.1.call-done = f32[16,512]{1,0:T(8,128)} async-done(((f32[2048,512]{1,0:T(8,128)}), f32[16,512]{1,0:T(8,128)}) %reduce-scatter.7.cloned.1.call-update) | async-done | bytes 32784
  1793.5 0.9 copy.30
  1794.4 18.3 psum.14
  1812.7 0.7 multiply_reduce_fusion
  1813.3 1.4 fusion.7
  1814.7 404.0 %psum.15 = f32[]{:T(128)} all-reduce(f32[]{:T(128)} %multiply_reduce_fusion), channel_id=1, replica_groups=mesh['grp'=6,'blk'=128] {'blk'}, use_global_device_ids=true, to_apply=%region_10.11 | all-reduce | flops 1 | bytes 8 | tf_op jit(solution)/shard_map/psum | solution.py:72
  2219.5 0.7 copy.28
  (27 shorter events, 0.2 us)
Async XLA Ops:
  7.2 4.1 copy-start
  7.2 5.6 copy-start.5
  7.2 137.9 %all-gather.2.cloned.1.call-start = ((), (), s32[]{:S(2)}) async-start(), calls=%async_computation.2 | async-start | bytes 1056768 | tf_op jit(solution)/shard_map/all_gather | solution.py:25
  9.6 966.2 %reduce-scatter.5.cloned.1.call-start = ((), (), s32[]{:S(2)}) async-start(), calls=%async_computation.3 | async-start | bytes 2113536 | tf_op jit(solution)/shard_map/reduce_scatter | solution.py:52
  146.9 10.1 copy-start.6
  158.1 0.7 copy-start.2
  158.8 2.0 copy-start.1
  160.7 1632.8 %reduce-scatter.7.cloned.1.call-start = ((), (), s32[]{:S(2)}) async-start(), calls=%async_computation.4 | async-start | bytes 4227072
  160.7 1.4 copy-start.3
  170.3 805.5 %copy-start.4 = (bf16[8,512]{1,0:T(8,128)(2,1)S(1)}, bf16[8,512]{1,0:T(8,128)(2,1)}, u32[]{:S(2)}) copy-start(bf16[8,512]{1,0:T(8,128)(2,1)} %param.7) | copy-start | bytes 24580
Sparse Core Ops, SparseCore 0:
  13.8 131.2 all-gather.1
  160.8 814.9 reduce-scatter.4
  979.2 814.2 reduce-scatter.6
where the time goes:
time: 2230 us
  waiting for transfers between devices  1750 us (78%)
  blocking collectives  422 us (19%)
    unnamed x4, waiting for transfers between devices  817 us
    reduce_scatter x1, waiting for transfers between devices, shards(): lax.psum_scatter(lax.dot_general(score_grad, query_unit, (((0,), (0,)), (...  805 us
    psum x1, blocking collectives, shards(): square_total = lax.psum(jnp.sum(weight_sum * weight_sum), 'blk')  404 us
    all_gather x1, waiting for transfers between devices, shards(): group_items = lax.all_gather(item_unit, 'blk', axis=0, tiled=True)  132 us
  transfers between devices with their start and end apart: 3, of which 3 were waited for; matrix products, arithmetic and copies ran while one was open for 1% of the time, Pallas kernels for 0%

commit v1 on v0

v1 whole, which is shorter than its diff:
```python
import functools

import jax
import jax.numpy as jnp
from jax import lax
from jax.experimental import pallas as pl
from jax.experimental.pallas import tpu as pltpu
from jax.sharding import PartitionSpec as P

MESH = pl.DeviceIdType.MESH
F32, BF16 = jnp.float32, jnp.bfloat16
INV_TAU = 50.0
EPSILON = 1e-06

NX, NY, NH, NL, NC = 4, 8, 4, 3, 2


def mod(value, size):
    return lax.rem(value + size, size)


def kernel(sizes, hid_hbm, proj_hbm, item_ref, pos_ref, hard_ref, ig_ref, wu_ref, s):
    nx, ny, nh, nl, nc = sizes
    q, hid = hid_hbm.shape
    emb = proj_hbm.shape[1]
    ipd = item_ref.shape[0]
    half = emb // 2
    wpd = wu_ref.shape[0]
    yr, ic = nh * ipd, ny * nh * ipd
    wyr, wc = nh * wpd, ny * nh * wpd

    grp, blk = lax.axis_index("grp"), lax.axis_index("blk")
    x, y, h = blk // (ny * nh), (blk // nh) % ny, blk % nh
    l, c = grp // nc, grp % nc

    def at(dx=0, dy=0, dh=0, dl=0, dc=0):
        place = (mod(x + dx, nx) * ny + mod(y + dy, ny)) * nh + mod(h + dh, nh)
        return (mod(l + dl, nl) * nc + mod(c + dc, nc), place)

    started = []

    def send(src, dst, device):
        i = len(started)
        copy = pltpu.make_async_remote_copy(
            src_ref=src,
            dst_ref=dst,
            send_sem=s["send"].at[i],
            recv_sem=s["recv"].at[i],
            device_id=device,
            device_id_type=MESH,
        )
        copy.start()
        started.append(copy)
        return copy

    partners = [at(dx=d) for d in range(1, nx)]
    partners += [at(dy=d) for d in range(1, ny)]
    partners += [at(dh=d) for d in range(1, nh)]
    others = [(dl, dc) for dl in range(nl) for dc in range(nc) if (dl, dc) != (0, 0)]
    partners += [at(dl=dl, dc=dc) for dl, dc in others]
    left, right, twin = at(dx=-1), at(dx=1), at(dc=1)

    barrier = pltpu.get_barrier_semaphore()
    for device in partners:
        pl.semaphore_signal(barrier, inc=1, device_id=device, device_id_type=MESH)
    load_proj = pltpu.make_async_copy(proj_hbm, s["proj"], s["local"].at[0])
    load_proj.start()
    load_hid = pltpu.make_async_copy(hid_hbm, s["h2"].at[pl.ds(0, q)], s["local"].at[1])
    load_hid.start()

    item = item_ref[...].astype(F32)
    item_inv = lax.rsqrt(jnp.sum(item * item, axis=-1, keepdims=True) + EPSILON)
    item_dir = item * item_inv
    s["hbuf"][0] = jnp.concatenate([item_dir[:, :half], item_dir[:, half:]], axis=0).astype(BF16)

    pl.semaphore_wait(barrier, len(partners))
    got_h = [send(s["hbuf"].at[0], s["hbuf"].at[d], at(dh=d)) for d in range(1, nh)]
    got_hid = send(hid_hbm, s["h2"].at[pl.ds(q, q)], twin)

    load_hid.wait()
    load_proj.wait()
    raw = jnp.dot(s["h2"][pl.ds(0, q), :], s["proj"][...], preferred_element_type=F32)
    query_inv = lax.rsqrt(jnp.sum(raw * raw, axis=-1, keepdims=True) + EPSILON)
    s["qd"][...] = raw * query_inv
    s["qu"][...] = s["qd"][...].astype(BF16)
    s["qinv"][...] = jnp.broadcast_to(query_inv, s["qinv"].shape)

    for copy in got_h:
        copy.wait_recv()
    for d in range(nh):
        block = s["hbuf"][d].astype(F32)
        s["hrow"][pl.ds(d * ipd, ipd), :] = jnp.concatenate([block[:ipd], block[ipd:]], axis=1)
    g = s["g"]
    g[0, pl.ds(0, yr), :] = s["hrow"][...].astype(BF16)

    def piece(slot, d):
        return g.at[slot, pl.ds(d * yr, yr)]

    got_y = {d: send(piece(0, 0), piece(0, d), at(dy=d)) for d in range(1, ny)}
    from_left, from_right, from_far = {}, {}, {}

    def pass_on(d):
        from_left[d].wait_recv()
        if d % 2 == 0:
            from_far[d] = send(piece(1, d), piece(2, d), right)
        from_right[d].wait_recv()
        if d % 2 == 1:
            from_far[d] = send(piece(3, d), piece(2, d), left)

    for d in range(ny):
        if d:
            got_y[d].wait_recv()
        from_left[d] = send(piece(0, d), piece(1, d), right)
        from_right[d] = send(piece(0, d), piece(3, d), left)
        if d == 0:
            s["h2t"][:, pl.ds(0, q)] = s["h2"][pl.ds(0, q), :].T
        if d >= 2:
            pass_on(d - 2)
    for d in range(max(ny - 2, 0), ny):
        pass_on(d)

    def column(ids):
        i, p = ids % ipd, ids // ipd
        hh, p = p % nh, p // nh
        yy, xx = p % ny, p // ny
        return ((mod(x - xx, nx) * ny + mod(y - yy, ny)) * nh + mod(h - hh, nh)) * ipd + i

    pos = column(jnp.broadcast_to(pos_ref[...], (q, q)).T[:, :1])
    ids = [pos] + [
        column(jnp.broadcast_to(hard_ref[k : k + 1, :], (q, q)).T[:, :1])
        for k in range(hard_ref.shape[0])
    ]
    lane = lax.broadcasted_iota(jnp.int32, (q, ic), 1)
    total = jnp.zeros((q, 1), F32)
    picks = [jnp.zeros((q, 1), F32) for _ in ids]
    for slot in (0, 1, 3, 2):
        if slot == 2:
            for d in range(ny):
                from_far[d].wait_recv()
        scores = lax.dot_general(
            s["qu"][...], g[slot], (((1,), (1,)), ((), ())), preferred_element_type=F32
        )
        e = jnp.exp(scores * INV_TAU)
        s["e"][slot] = e
        total = total + jnp.sum(e, axis=1, keepdims=True)
        for k, column_of in enumerate(ids):
            hit = lane == column_of - slot * ic
            picks[k] = picks[k] + jnp.sum(jnp.where(hit, e, 0.0), axis=1, keepdims=True)

    weights = [pick / (pick + picks[0]) for pick in picks[1:]]
    extra = 1.0 + functools.reduce(jnp.add, weights)
    inverse = 1.0 / total
    query_grad = jnp.zeros((q, emb), F32)
    for slot in range(nx):
        grad = s["e"][slot] * inverse
        for k, column_of in enumerate(ids):
            hit = lane == column_of - slot * ic
            grad = grad + jnp.where(hit, -extra if k == 0 else weights[k - 1], 0.0)
        s["sg"][slot] = (grad * INV_TAU).astype(BF16)
        query_grad = query_grad + jnp.dot(s["sg"][slot], g[slot], preferred_element_type=F32)

    query_dir = s["qd"][...]
    inner = jnp.sum(query_dir * query_grad, axis=-1, keepdims=True)
    raw_grad = (s["qinv"][:, :1] * (query_grad - query_dir * inner)).astype(BF16)
    s["raw"][0] = raw_grad[:, :half]
    s["raw"][1] = raw_grad[:, half:]
    got_raw = send(s["raw"].at[mod(c + 1, nc)], s["raw2"].at[pl.ds(q, q)], twin)
    s["raw2"][pl.ds(0, q), :] = s["raw"][c]

    got_hid.wait_recv()
    s["h2t"][:, pl.ds(q, q)] = s["h2"][pl.ds(q, q), :].T

    def parts(name, term, rows):
        n = rows // 2
        a, b = pl.ds(0, n), pl.ds(n, n)
        own, far, to_right, to_left, in_a, in_b, in_left, in_right = (
            s[name + "_" + key] for key in ("own", "far", "tr", "tl", "ia", "ib", "il", "ir")
        )
        keep_a, keep_b = s[name + "_ka"], s[name + "_kb"]
        out = {}

        def fill():
            far[...] = term(2).astype(BF16)
            value = term(3)
            keep_a[...] = value[:n]
            to_right[b, :] = value[n:].astype(BF16)
            value = term(1)
            keep_b[...] = value[n:]
            to_left[a, :] = value[:n].astype(BF16)
            own[...] = term(0)

        def first():
            out["a"] = send(far.at[a], in_a, right)
            out["b"] = send(far.at[b], in_b, left)
            out["rb"] = send(to_right.at[b], in_left.at[b], right)
            out["la"] = send(to_left.at[a], in_right.at[a], left)

        def second():
            out["a"].wait_recv()
            to_right[a, :] = (keep_a[...] + in_a[...].astype(F32)).astype(BF16)
            out["ra"] = send(to_right.at[a], in_left.at[a], right)
            out["b"].wait_recv()
            to_left[b, :] = (keep_b[...] + in_b[...].astype(F32)).astype(BF16)
            out["lb"] = send(to_left.at[b], in_right.at[b], left)

        def last():
            for key in ("rb", "la", "ra", "lb"):
                out[key].wait_recv()
            value = own[...] + in_left[...].astype(F32) + in_right[...].astype(F32)
            own[...] = value
            s[name + "_sum"][...] = value.astype(BF16)

        return fill, first, second, last

    def unit_term(slot):
        return lax.dot_general(
            s["sg"][slot], s["qu"][...], (((0,), (0,)), ((), ())), preferred_element_type=F32
        )

    def weight_term(slot):
        rows = pl.ds(pl.multiple_of(mod(x - slot, nx) * wc, wc), wc)
        return jnp.dot(s["h2t"][rows, :], s["raw2"][...], preferred_element_type=F32)

    u_fill, u_first, u_second, u_last = parts("u", unit_term, ic)
    w_fill, w_first, w_second, w_last = parts("w", weight_term, wc)
    u_fill()
    got_raw.wait_recv()
    w_fill()
    w_first()
    w_second()
    w_last()

    def weight_rows(d):
        return pl.ds(pl.multiple_of(mod(y - d, ny) * wyr, wyr), wyr)

    got_wy = [
        send(s["w_sum"].at[weight_rows(d)], s["wy"].at[d], at(dy=-d)) for d in range(1, ny)
    ]
    u_first()
    value = s["w_own"][weight_rows(0), :]
    for d, copy in enumerate(got_wy, 1):
        copy.wait_recv()
        value = value + s["wy"][d].astype(F32)
    s["wyf"][...] = value

    def weight_block(d):
        return pl.ds(pl.multiple_of(mod(h - d, nh) * wpd, wpd), wpd)

    got_wh = [send(s["wyf"].at[weight_block(d)], s["wh"].at[d], at(dh=-d)) for d in range(1, nh)]
    u_second()
    value = s["wyf"][weight_block(0), :]
    for d, copy in enumerate(got_wh, 1):
        copy.wait_recv()
        value = value + s["wh"][d]
    lc = s["lc"]
    lc[grp] = value
    got_lc = [send(lc.at[grp], lc.at[grp], at(dl=dl, dc=dc)) for dl, dc in others]
    for copy in got_lc:
        copy.wait_recv()
    sides = [functools.reduce(jnp.add, [lc[i * nc + j] for i in range(nl)]) for j in range(nc)]
    weight_sum = jnp.concatenate(sides, axis=1)

    def spread(name, size, value, key):
        buffer = s[name]
        buffer[0] = value
        return [send(buffer.at[0], buffer.at[d], at(**{key: d})) for d in range(1, size)]

    def gather(name, size, copies):
        for copy in copies:
            copy.wait_recv()
        return functools.reduce(jnp.add, [s[name][d] for d in range(size)])

    square = jnp.broadcast_to(jnp.sum(weight_sum * weight_sum, keepdims=True), (8, 128))
    got_sq = spread("sqy", ny, square, "dy")
    u_last()
    got_uy = [
        send(s["u_sum"].at[pl.ds(d * yr, yr)], s["uy"].at[d], at(dy=-d)) for d in range(1, ny)
    ]
    square = gather("sqy", ny, got_sq)
    got_sq = spread("sqh", nh, square, "dh")
    square = gather("sqh", nh, got_sq)
    got_sq = spread("sqx", nx, square, "dx")
    value = s["u_own"][pl.ds(0, yr), :]
    for d, copy in enumerate(got_uy, 1):
        copy.wait_recv()
        value = value + s["uy"][d].astype(F32)
    s["uyf"][...] = value
    got_uh = [
        send(s["uyf"].at[pl.ds(d * ipd, ipd)], s["uh"].at[d], at(dh=-d)) for d in range(1, nh)
    ]
    square = gather("sqx", nx, got_sq)
    mean = square[:1, :1] / (hid * emb)
    wu_ref[...] = weight_sum * lax.rsqrt(mean + EPSILON)
    value = s["uyf"][pl.ds(0, ipd), :]
    for d, copy in enumerate(got_uh, 1):
        copy.wait_recv()
        value = value + s["uh"][d]
    inner = jnp.sum(item_dir * value, axis=-1, keepdims=True)
    ig_ref[...] = item_inv * (value - item_dir * inner)
    for copy in started:
        copy.wait_send()


def ring_scratch(name, rows, cols):
    n = rows // 2
    shapes = {"own": ((rows, cols), F32), "ka": ((n, cols), F32), "kb": ((n, cols), F32)}
    shapes |= {key: ((rows, cols), BF16) for key in ("far", "tr", "tl", "il", "ir", "sum")}
    shapes |= {key: ((n, cols), BF16) for key in ("ia", "ib")}
    return {name + "_" + key: pltpu.VMEM(*shape) for key, shape in shapes.items()}


def step(sizes, query_hidden, query_proj, item_embed, positive, hard_ids):
    nx, ny, nh, nl, nc = sizes
    q, hid = query_hidden.shape
    emb, ipd = query_proj.shape[1], item_embed.shape[0]
    half, wpd = emb // 2, hid // (nx * ny * nh)
    yr, ic = nh * ipd, ny * nh * ipd
    wyr, wc = nh * wpd, ny * nh * wpd
    copies = 128
    scratch = {
        "proj": pltpu.VMEM((hid, emb), BF16),
        "h2": pltpu.VMEM((2 * q, hid), BF16),
        "h2t": pltpu.VMEM((hid, 2 * q), BF16),
        "hbuf": pltpu.VMEM((nh, 2 * ipd, half), BF16),
        "hrow": pltpu.VMEM((yr, emb), F32),
        "g": pltpu.VMEM((nx, ic, emb), BF16),
        "qd": pltpu.VMEM((q, emb), F32),
        "qu": pltpu.VMEM((q, emb), BF16),
        "qinv": pltpu.VMEM((q, 128), F32),
        "e": pltpu.VMEM((nx, q, ic), F32),
        "sg": pltpu.VMEM((nx, q, ic), BF16),
        "raw": pltpu.VMEM((2, q, half), BF16),
        "raw2": pltpu.VMEM((2 * q, half), BF16),
        "wy": pltpu.VMEM((ny, wyr, half), BF16),
        "wyf": pltpu.VMEM((wyr, half), F32),
        "wh": pltpu.VMEM((nh, wpd, half), F32),
        "lc": pltpu.VMEM((nl * nc, wpd, half), F32),
        "uy": pltpu.VMEM((ny, yr, emb), BF16),
        "uyf": pltpu.VMEM((yr, emb), F32),
        "uh": pltpu.VMEM((nh, ipd, emb), F32),
        "sqy": pltpu.VMEM((ny, 8, 128), F32),
        "sqh": pltpu.VMEM((nh, 8, 128), F32),
        "sqx": pltpu.VMEM((nx, 8, 128), F32),
        "send": pltpu.SemaphoreType.DMA((copies,)),
        "recv": pltpu.SemaphoreType.DMA((copies,)),
        "local": pltpu.SemaphoreType.DMA((2,)),
    }
    scratch |= ring_scratch("u", ic, emb)
    scratch |= ring_scratch("w", wc, half)
    names = list(scratch)

    def body(*refs):
        kernel(sizes, *refs[:7], dict(zip(names, refs[7:])))

    vmem = pl.BlockSpec(memory_space=pltpu.VMEM)
    anywhere = pl.BlockSpec(memory_space=pl.ANY)
    return pl.pallas_call(
        body,
        out_shape=(
            jax.ShapeDtypeStruct((ipd, emb), F32),
            jax.ShapeDtypeStruct((wpd, emb), F32),
        ),
        in_specs=[anywhere, anywhere, vmem, vmem, vmem],
        out_specs=(vmem, vmem),
        scratch_shapes=list(scratch.values()),
        compiler_params=pltpu.CompilerParams(
            collective_id=0, has_side_effects=True, vmem_limit_bytes=48 * 2**20
        ),
    )(query_hidden, query_proj, item_embed, positive.reshape(1, q), hard_ids.T)


def solution(mesh):
    return jax.shard_map(
        functools.partial(step, (NX, NY, NH, NL, NC)),
        mesh=mesh,
        in_specs=(
            P(("grp", "blk"), None),
            P(),
            P(("grp", "blk"), None),
            P(("grp", "blk")),
            P(("grp", "blk"), None),
        ),
        out_specs=(P(("grp", "blk"), None), P("blk", None)),
        check_vma=False,
    )
```

time: 2230 us -> 102 us (0.05)
  the two profiles are of different devices: /device:TPU:64 before, /device:TPU:1 now
where the time goes in v1:
time: 102 us; the launch traced here: 99.9 us
  Pallas kernels  93.4 us (92%)
  local copies, waits for them, and re-layouts  5.88 us (6%)
    pallas_call x1, Pallas kernels, step(): pl.pallas_call(body, out_shape=(jax.ShapeDtypeStruct((ipd, emb), F32), ja...  93.4 us
    unnamed x12, local copies, waits for them, and re-layouts  5.88 us

profile of v1, /device:TPU:1, one launch (start us, length us, event | category | flops | bytes accessed | tf_op | source)
XLA Modules:
  0.0 99.9 jit_solution(18018775271783037465)
XLA Ops:
  0.6 0.0 copy-start
  0.6 1.6 %copy-done = bf16[2048,512]{1,0:T(8,128)(2,1)S(1)} copy-done((bf16[2048,512]{1,0:T(8,128)(2,1)S(1)}, bf16[2048,512]{1,0:T(8,128)(2,1)}, u32[]{:S(2)}) %copy-start) | copy-done | bytes 2097176
  2.2 0.0 copy-start.1
  2.2 1.0 %copy-done.1 = bf16[128,2048]{1,0:T(8,128)(2,1)S(1)} copy-done((bf16[128,2048]{1,0:T(8,128)(2,1)S(1)}, bf16[128,2048]{1,0:T(8,128)(2,1)}, u32[]{:S(2)}) %copy-start.1) | copy-done | bytes 524312
  3.3 0.0 copy-start.2
  3.3 0.7 copy-done.2
  4.0 0.0 copy-start.3
  4.0 0.7 copy-done.3
  4.7 0.0 copy-start.4
  4.7 0.7 copy-done.4
  5.3 93.4 %shard_map.68 = (f32[8,512]{1,0:T(8,128)S(1)}, f32[16,512]{1,0:T(8,128)S(1)}) custom-call(bf16[128,2048]{1,0:T(8,128)(2,1)S(1)} %copy-done.1, bf16[2048,512]{1,0:T(8,128)(2,1)S(1)} %copy-done, bf16[8,512]{1,0:T(8,128)(2,1)S(1)} %copy-done.2, s32[1,128]{1,0:T(1,128)S(1)} %bitcast.3, s32[8,128]{1,0:T(8,128)S(1)} %bitcast.2), custom_call_target="tpu_custom_call" | custom-call | tf_op jit(solution)/shard_map/pallas_call | solution.py:357
  98.7 0.6 copy.9
  99.3 0.6 copy.10
Async XLA Ops:
  0.6 1.6 %copy-start = (bf16[2048,512]{1,0:T(8,128)(2,1)S(1)}, bf16[2048,512]{1,0:T(8,128)(2,1)}, u32[]{:S(2)}) copy-start(bf16[2048,512]{1,0:T(8,128)(2,1)} %refs_1_.1) | copy-start | bytes 6291460
  2.2 1.0 %copy-start.1 = (bf16[128,2048]{1,0:T(8,128)(2,1)S(1)}, bf16[128,2048]{1,0:T(8,128)(2,1)}, u32[]{:S(2)}) copy-start(bf16[128,2048]{1,0:T(8,128)(2,1)} %refs_0_.1) | copy-start | bytes 1572868
  3.3 0.7 copy-start.2
  4.0 0.7 copy-start.3
  4.7 0.7 copy-start.4

commit v2 on v1

v2 whole, which is shorter than its diff:
```python
import functools

import jax
import jax.numpy as jnp
from jax import lax
from jax.experimental import pallas as pl
from jax.experimental.pallas import tpu as pltpu
from jax.sharding import PartitionSpec as P

MESH = pl.DeviceIdType.MESH
F32, BF16 = jnp.float32, jnp.bfloat16
INV_TAU = 50.0
EPSILON = 1e-06

NX, NY, NH, NL, NC = 4, 8, 4, 3, 2


def mod(value, size):
    return lax.rem(value + size, size)


def kernel(sizes, hid_hbm, proj_hbm, item_hbm, pos_hbm, hard_hbm, ig_ref, wu_ref, s):
    nx, ny, nh, nl, nc = sizes
    q, hid = hid_hbm.shape
    emb = proj_hbm.shape[1]
    ipd = item_hbm.shape[0]
    half = emb // 2
    wpd = wu_ref.shape[0]
    yr, ic = nh * ipd, ny * nh * ipd
    wyr, wc = nh * wpd, ny * nh * wpd

    grp, blk = lax.axis_index("grp"), lax.axis_index("blk")
    x, y, h = blk // (ny * nh), (blk // nh) % ny, blk % nh
    l, c = grp // nc, grp % nc

    def at(dx=0, dy=0, dh=0, dl=0, dc=0):
        place = (mod(x + dx, nx) * ny + mod(y + dy, ny)) * nh + mod(h + dh, nh)
        return (mod(l + dl, nl) * nc + mod(c + dc, nc), place)

    started = []

    def send(src, dst, device):
        i = len(started)
        copy = pltpu.make_async_remote_copy(
            src_ref=src,
            dst_ref=dst,
            send_sem=s["send"].at[i],
            recv_sem=s["recv"].at[i],
            device_id=device,
            device_id_type=MESH,
        )
        copy.start()
        started.append(copy)
        return copy

    across = [(dx, dh) for dx in range(nx) for dh in range(nh) if (dx, dh) != (0, 0)]
    along = [(dh, dl) for dh in range(nh) for dl in range(nl) if (dh, dl) != (0, 0)]
    partners = [at(dx=dx, dh=dh) for dx, dh in across]
    partners += [at(dy=d) for d in range(1, ny)]
    partners += [at(dh=dh, dl=dl) for dh, dl in along if dl]
    partners += [at(dx=d, dc=1) for d in range(nx)]
    left, right, far, twin = at(dx=-1), at(dx=1), at(dx=2), at(dc=1)

    barrier = pltpu.get_barrier_semaphore()
    for device in partners:
        pl.semaphore_signal(barrier, inc=1, device_id=device, device_id_type=MESH)

    def load(src, dst, i):
        copy = pltpu.make_async_copy(src, dst, s["local"].at[i])
        copy.start()
        return copy

    def hid_columns(d):
        return hid_hbm.at[:, pl.ds(pl.multiple_of(mod(x + d, nx) * wc, wc), wc)]

    load_item = load(item_hbm, s["item"], 0)
    load_hid = load(hid_hbm, s["hq"], 1)
    load_proj = load(proj_hbm, s["proj"], 2)
    load_own = load(hid_columns(0), s["hx"].at[0, pl.ds(0, q)], 3)
    load_pos = load(pos_hbm, s["pos"], 4)
    load_hard = load(hard_hbm, s["hard"], 5)

    load_item.wait()
    item = s["item"][...].astype(F32)
    item_inv = lax.rsqrt(jnp.sum(item * item, axis=-1, keepdims=True) + EPSILON)
    item_dir = item * item_inv
    s["hbuf"][0] = jnp.concatenate([item_dir[:, :half], item_dir[:, half:]], axis=0).astype(BF16)

    pl.semaphore_wait(barrier, len(partners))
    got_h = [send(s["hbuf"].at[0], s["hbuf"].at[d], at(dh=d)) for d in range(1, nh)]
    got_hx = [
        send(hid_columns(d), s["hx"].at[d, pl.ds(0, q)], at(dx=d)) for d in range(1, nx)
    ]

    load_hid.wait()
    load_proj.wait()
    raw = jnp.dot(s["hq"][...], s["proj"][...], preferred_element_type=F32)
    query_inv = lax.rsqrt(jnp.sum(raw * raw, axis=-1, keepdims=True) + EPSILON)
    s["qd"][...] = raw * query_inv
    qx = s["qx"]
    qx[pl.ds(0, q), :] = s["qd"][...].astype(BF16)
    s["qinv"][...] = jnp.broadcast_to(query_inv, s["qinv"].shape)

    for copy in got_h:
        copy.wait_recv()
    for d in range(nh):
        block = s["hbuf"][d].astype(F32)
        s["hrow"][pl.ds(d * ipd, ipd), :] = jnp.concatenate([block[:ipd], block[ipd:]], axis=1)
    g = s["g"]
    g[0, pl.ds(0, yr), :] = s["hrow"][...].astype(BF16)

    def piece(slot, d):
        return g.at[slot, pl.ds(d * yr, yr)]

    got_y = {d: send(piece(0, 0), piece(0, d), at(dy=d)) for d in range(1, ny)}
    from_left, from_right, from_far = {}, {}, {}

    order = sorted(range(ny), key=lambda d: (min(d, ny - d), d))
    relayed = max(ny - 3, 1)

    def pass_on(i):
        d = order[i]
        from_left[d].wait_recv()
        if i < relayed and i % 2 == 0:
            from_far[d] = send(piece(1, d), piece(2, d), right)
        from_right[d].wait_recv()
        if i < relayed and i % 2 == 1:
            from_far[d] = send(piece(3, d), piece(2, d), left)

    for i, d in enumerate(order):
        if d:
            got_y[d].wait_recv()
        from_left[d] = send(piece(0, d), piece(1, d), right)
        from_right[d] = send(piece(0, d), piece(3, d), left)
        if i >= relayed:
            from_far[d] = send(piece(0, d), piece(2, d), far)
        if i == min(2, ny - 1):
            for copy in got_hx:
                copy.wait_recv()
            load_own.wait()
            got_hid = send(s["hx"].at[:, pl.ds(0, q)], s["hx"].at[:, pl.ds(q, q)], twin)
        if i >= 2:
            pass_on(i - 2)
    got_qx = [send(qx.at[pl.ds(0, q)], qx.at[pl.ds(d * q, q)], at(dx=d)) for d in range(1, nx)]

    def column(ids):
        i, p = ids % ipd, ids // ipd
        hh, p = p % nh, p // nh
        yy, xx = p % ny, p // ny
        return ((mod(x - xx, nx) * ny + mod(y - yy, ny)) * nh + mod(h - hh, nh)) * ipd + i

    load_pos.wait()
    load_hard.wait()
    pos_ref, hard_ref = s["pos"], s["hard"]
    pos = column(jnp.broadcast_to(pos_ref[...], (q, q)).T[:, :1])
    ids = [pos] + [
        column(jnp.broadcast_to(hard_ref[k : k + 1, :], (q, q)).T[:, :1])
        for k in range(hard_ref.shape[0])
    ]
    lane = lax.broadcasted_iota(jnp.int32, (q, ic), 1)
    total = jnp.zeros((q, 1), F32)
    picks = [jnp.zeros((q, 1), F32) for _ in ids]
    for slot in (0, 1, 3, 2):
        if slot == 1:
            for i in range(max(ny - 2, 0), ny):
                pass_on(i)
        if slot == 2:
            for d in range(ny):
                from_far[d].wait_recv()
        scores = lax.dot_general(
            qx[pl.ds(0, q), :], g[slot], (((1,), (1,)), ((), ())), preferred_element_type=F32
        )
        e = jnp.exp(scores * INV_TAU)
        s["e"][slot] = e
        total = total + jnp.sum(e, axis=1, keepdims=True)
        for k, column_of in enumerate(ids):
            hit = lane == column_of - slot * ic
            picks[k] = picks[k] + jnp.sum(jnp.where(hit, e, 0.0), axis=1, keepdims=True)

    weights = [pick / (pick + picks[0]) for pick in picks[1:]]
    extra = 1.0 + functools.reduce(jnp.add, weights)
    inverse = 1.0 / total
    query_grad = jnp.zeros((q, emb), F32)
    for slot in range(nx):
        grad = s["e"][slot] * inverse
        for k, column_of in enumerate(ids):
            hit = lane == column_of - slot * ic
            grad = grad + jnp.where(hit, -extra if k == 0 else weights[k - 1], 0.0)
        s["sg"][slot] = (grad * INV_TAU).astype(BF16)
        query_grad = query_grad + jnp.dot(s["sg"][slot], g[slot], preferred_element_type=F32)

    query_dir = s["qd"][...]
    inner = jnp.sum(query_dir * query_grad, axis=-1, keepdims=True)
    raw_grad = (s["qinv"][:, :1] * (query_grad - query_dir * inner)).astype(BF16)
    s["raw"][0] = raw_grad[:, :half]
    s["raw"][1] = raw_grad[:, half:]
    rx = s["rx"]
    mine, other = s["raw"].at[c], s["raw"].at[mod(c + 1, nc)]
    got_rx = {0: [], 1: [], 2: [], 3: []}
    for d in (1, 3, 2, 0):
        if d:
            got_rx[d].append(send(mine, rx.at[d, pl.ds(0, q)], at(dx=d)))
        got_rx[d].append(send(other, rx.at[d, pl.ds(q, q)], at(dx=d, dc=1)))
    sgx = s["sgx"]
    got_sg = [
        send(s["sg"].at[d], sgx.at[pl.ds((nx - d) * q, q)], at(dx=-d)) for d in range(1, nx)
    ]
    rx[0, pl.ds(0, q), :] = s["raw"][c]
    sgx[pl.ds(0, q), :] = s["sg"][0]
    got_hid.wait_recv()
    for d in range(nx):
        s["hxt"][d] = s["hx"][d].T
    value = jnp.zeros((wc, half), F32)
    for d in (0, 1, 3, 2):
        for copy in got_rx[d]:
            copy.wait_recv()
        value = value + jnp.dot(s["hxt"][d], rx[d], preferred_element_type=F32)
    s["w_own"][...] = value
    s["w_sum"][...] = value.astype(BF16)

    def weight_rows(d):
        return pl.ds(pl.multiple_of(mod(y - d, ny) * wyr, wyr), wyr)

    near = order[1:]
    got_wy = {d: send(s["w_sum"].at[weight_rows(d)], s["wy"].at[d], at(dy=-d)) for d in near}
    for copy in got_sg + got_qx:
        copy.wait_recv()
    value = lax.dot_general(sgx[...], qx[...], (((0,), (0,)), ((), ())), preferred_element_type=F32)
    s["u_own"][...] = value[:yr]
    s["u_sum"][...] = value.astype(BF16)
    value = s["w_own"][weight_rows(0), :]
    for d in near:
        got_wy[d].wait_recv()
        value = value + s["wy"][d].astype(F32)
    s["wyb"][...] = value.astype(BF16)

    def weight_block(d):
        return pl.ds(pl.multiple_of(mod(h - d, nh) * wpd, wpd), wpd)

    wz = s["wz"]
    got_wz = [
        send(s["wyb"].at[weight_block(dh)], wz.at[dh * nl + l], at(dh=-dh, dl=-dl))
        for dh, dl in along
    ]
    got_uy = {
        d: send(s["u_sum"].at[pl.ds(d * yr, yr)], s["uy"].at[d], at(dy=-d)) for d in near
    }
    wz[l] = s["wyb"][weight_block(0), :]
    for copy in got_wz:
        copy.wait_recv()
    value = functools.reduce(jnp.add, [wz[i].astype(F32) for i in range(nh * nl)])
    lc = s["lc"]
    lc[c] = value
    send(lc.at[c], lc.at[c], twin).wait_recv()
    weight_sum = jnp.concatenate([lc[0], lc[1]], axis=1)

    def spread(name, value, devices):
        buffer = s[name]
        buffer[0] = value
        return [send(buffer.at[0], buffer.at[i], device) for i, device in enumerate(devices, 1)]

    def gather(name, copies):
        for copy in copies:
            copy.wait_recv()
        return functools.reduce(jnp.add, [s[name][i] for i in range(len(copies) + 1)])

    square = jnp.broadcast_to(jnp.sum(weight_sum * weight_sum, keepdims=True), (8, 128))
    got_sq = spread("sqy", square, [at(dy=d) for d in range(1, ny)])
    value = s["u_own"][...]
    for d in near:
        got_uy[d].wait_recv()
        value = value + s["uy"][d].astype(F32)
    s["uyf"][...] = value
    square = gather("sqy", got_sq)
    got_sq = spread("sqxh", square, [at(dx=dx, dh=dh) for dx, dh in across])
    got_uh = [
        send(s["uyf"].at[pl.ds(d * ipd, ipd)], s["uh"].at[d], at(dh=-d)) for d in range(1, nh)
    ]
    square = gather("sqxh", got_sq)
    mean = square[:1, :1] / (hid * emb)
    wu_ref[...] = weight_sum * lax.rsqrt(mean + EPSILON)
    value = s["uyf"][pl.ds(0, ipd), :]
    for d, copy in enumerate(got_uh, 1):
        copy.wait_recv()
        value = value + s["uh"][d]
    inner = jnp.sum(item_dir * value, axis=-1, keepdims=True)
    ig_ref[...] = item_inv * (value - item_dir * inner)
    for copy in started:
        copy.wait_send()


def step(sizes, query_hidden, query_proj, item_embed, positive, hard_ids):
    nx, ny, nh, nl, nc = sizes
    q, hid = query_hidden.shape
    emb, ipd = query_proj.shape[1], item_embed.shape[0]
    half, wpd = emb // 2, hid // (nx * ny * nh)
    yr, ic = nh * ipd, ny * nh * ipd
    wyr, wc = nh * wpd, ny * nh * wpd
    copies = 128
    scratch = {
        "proj": pltpu.VMEM((hid, emb), BF16),
        "item": pltpu.VMEM((ipd, emb), BF16),
        "pos": pltpu.VMEM((1, q), jnp.int32),
        "hard": pltpu.VMEM((hard_ids.shape[1], q), jnp.int32),
        "hq": pltpu.VMEM((q, hid), BF16),
        "hx": pltpu.VMEM((nx, nc * q, wc), BF16),
        "hxt": pltpu.VMEM((nx, wc, nc * q), BF16),
        "hbuf": pltpu.VMEM((nh, 2 * ipd, half), BF16),
        "hrow": pltpu.VMEM((yr, emb), F32),
        "g": pltpu.VMEM((nx, ic, emb), BF16),
        "qd": pltpu.VMEM((q, emb), F32),
        "qx": pltpu.VMEM((nx * q, emb), BF16),
        "qinv": pltpu.VMEM((q, 128), F32),
        "e": pltpu.VMEM((nx, q, ic), F32),
        "sg": pltpu.VMEM((nx, q, ic), BF16),
        "sgx": pltpu.VMEM((nx * q, ic), BF16),
        "raw": pltpu.VMEM((nc, q, half), BF16),
        "rx": pltpu.VMEM((nx, nc * q, half), BF16),
        "w_own": pltpu.VMEM((wc, half), F32),
        "w_sum": pltpu.VMEM((wc, half), BF16),
        "wy": pltpu.VMEM((ny, wyr, half), BF16),
        "wyb": pltpu.VMEM((wyr, half), BF16),
        "wz": pltpu.VMEM((nh * nl, wpd, half), BF16),
        "lc": pltpu.VMEM((nc, wpd, half), F32),
        "u_own": pltpu.VMEM((yr, emb), F32),
        "u_sum": pltpu.VMEM((ic, emb), BF16),
        "uy": pltpu.VMEM((ny, yr, emb), BF16),
        "uyf": pltpu.VMEM((yr, emb), F32),
        "uh": pltpu.VMEM((nh, ipd, emb), F32),
        "sqy": pltpu.VMEM((ny, 8, 128), F32),
        "sqxh": pltpu.VMEM((nx * nh, 8, 128), F32),
        "send": pltpu.SemaphoreType.DMA((copies,)),
        "recv": pltpu.SemaphoreType.DMA((copies,)),
        "local": pltpu.SemaphoreType.DMA((6,)),
    }
    names = list(scratch)

    def body(*refs):
        kernel(sizes, *refs[:7], dict(zip(names, refs[7:])))

    vmem = pl.BlockSpec(memory_space=pltpu.VMEM)
    anywhere = pl.BlockSpec(memory_space=pltpu.HBM)
    return pl.pallas_call(
        body,
        out_shape=(
            jax.ShapeDtypeStruct((ipd, emb), F32),
            jax.ShapeDtypeStruct((wpd, emb), F32),
        ),
        in_specs=[anywhere] * 5,
        out_specs=(vmem, vmem),
        scratch_shapes=list(scratch.values()),
        compiler_params=pltpu.CompilerParams(
            collective_id=0, has_side_effects=True, vmem_limit_bytes=63 * 2**20
        ),
    )(query_hidden, query_proj, item_embed, positive.reshape(1, q), hard_ids.T)


def solution(mesh):
    return jax.shard_map(
        functools.partial(step, (NX, NY, NH, NL, NC)),
        mesh=mesh,
        in_specs=(
            P(("grp", "blk"), None),
            P(),
            P(("grp", "blk"), None),
            P(("grp", "blk")),
            P(("grp", "blk"), None),
        ),
        out_specs=(P(("grp", "blk"), None), P("blk", None)),
        check_vma=False,
    )
```

time: 102 us -> 90.9 us (0.89)
  Pallas kernels: 93.4 us -> 86.4 us
  local copies, waits for them, and re-layouts: 5.88 us -> 2.7 us
    pallas_call x1, Pallas kernels: 93.4 us -> 86.4 us  [step(): pl.pallas_call(body, out_shape=(jax.ShapeDtypeStruct((ipd, emb), F32), ja...]
    unnamed x12 -> x2, local copies, waits for them, and re-layouts: 5.88 us -> 2.7 us
where the time goes in v2:
time: 90.9 us; the launch traced here: 89.7 us
  Pallas kernels  86.4 us (95%)
  local copies, waits for them, and re-layouts  2.7 us (3%)
    pallas_call x1, Pallas kernels, step(): pl.pallas_call(body, out_shape=(jax.ShapeDtypeStruct((ipd, emb), F32), ja...  86.4 us
    unnamed x2, local copies, waits for them, and re-layouts  2.7 us

profile of v2, /device:TPU:1, one launch (start us, length us, event | category | flops | bytes accessed | tf_op | source)
XLA Modules:
  0.0 89.7 jit_solution(4722904237784751522)
XLA Ops:
  0.6 86.4 %shard_map.68 = (f32[8,512]{1,0:T(8,128)}, f32[16,512]{1,0:T(8,128)}) custom-call(bf16[128,2048]{1,0:T(8,128)(2,1)} %refs_0_.1, bf16[2048,512]{1,0:T(8,128)(2,1)} %refs_1_.1, bf16[8,512]{1,0:T(8,128)(2,1)} %refs_2_.1, s32[1,128]{1,0:T(1,128)} %bitcast.3, s32[8,128]{1,0:T(8,128)} %bitcast.2), custom_call_target="tpu_custom_call" | custom-call | tf_op jit(solution)/shard_map/pallas_call | solution.py:343
  87.0 1.3 %copy.9 = f32[8,512]{1,0:T(8,128)} copy(f32[8,512]{1,0:T(8,128)} %get-tuple-element.4) | data formatting | bytes 32768
  88.3 1.4 %copy.10 = f32[16,512]{1,0:T(8,128)} copy(f32[16,512]{1,0:T(8,128)} %get-tuple-element.5) | data formatting | bytes 65536

commit v3 on v2

--- a/solution.py
+++ b/solution.py
@@ -55,10 +55,11 @@
 
     across = [(dx, dh) for dx in range(nx) for dh in range(nh) if (dx, dh) != (0, 0)]
     along = [(dh, dl) for dh in range(nh) for dl in range(nl) if (dh, dl) != (0, 0)]
-    partners = [at(dx=dx, dh=dh) for dx, dh in across]
+    partners = [at(dx=d) for d in range(1, nx)]
     partners += [at(dy=d) for d in range(1, ny)]
-    partners += [at(dh=dh, dl=dl) for dh, dl in along if dl]
-    partners += [at(dx=d, dc=1) for d in range(nx)]
+    partners += [at(dh=d) for d in range(1, nh)]
+    partners += [at(dl=d) for d in range(1, nl)]
+    partners += [at(dc=1)]
     left, right, far, twin = at(dx=-1), at(dx=1), at(dx=2), at(dc=1)
 
     barrier = pltpu.get_barrier_semaphore()
@@ -116,7 +117,7 @@
     from_left, from_right, from_far = {}, {}, {}
 
     order = sorted(range(ny), key=lambda d: (min(d, ny - d), d))
-    relayed = max(ny - 3, 1)
+    relayed, lag = max(ny // 2, 1), 4
 
     def pass_on(i):
         d = order[i]
@@ -139,9 +140,8 @@
                 copy.wait_recv()
             load_own.wait()
             got_hid = send(s["hx"].at[:, pl.ds(0, q)], s["hx"].at[:, pl.ds(q, q)], twin)
-        if i >= 2:
-            pass_on(i - 2)
-    got_qx = [send(qx.at[pl.ds(0, q)], qx.at[pl.ds(d * q, q)], at(dx=d)) for d in range(1, nx)]
+        if i >= lag:
+            pass_on(i - lag)
 
     def column(ids):
         i, p = ids % ipd, ids // ipd
@@ -162,7 +162,7 @@
     picks = [jnp.zeros((q, 1), F32) for _ in ids]
     for slot in (0, 1, 3, 2):
         if slot == 1:
-            for i in range(max(ny - 2, 0), ny):
+            for i in range(max(ny - lag, 0), ny):
                 pass_on(i)
         if slot == 2:
             for d in range(ny):
@@ -195,19 +195,14 @@
     s["raw"][0] = raw_grad[:, :half]
     s["raw"][1] = raw_grad[:, half:]
     rx = s["rx"]
+    got_hid.wait_recv()
     mine, other = s["raw"].at[c], s["raw"].at[mod(c + 1, nc)]
     got_rx = {0: [], 1: [], 2: [], 3: []}
     for d in (1, 3, 2, 0):
         if d:
             got_rx[d].append(send(mine, rx.at[d, pl.ds(0, q)], at(dx=d)))
         got_rx[d].append(send(other, rx.at[d, pl.ds(q, q)], at(dx=d, dc=1)))
-    sgx = s["sgx"]
-    got_sg = [
-        send(s["sg"].at[d], sgx.at[pl.ds((nx - d) * q, q)], at(dx=-d)) for d in range(1, nx)
-    ]
     rx[0, pl.ds(0, q), :] = s["raw"][c]
-    sgx[pl.ds(0, q), :] = s["sg"][0]
-    got_hid.wait_recv()
     for d in range(nx):
         s["hxt"][d] = s["hx"][d].T
     value = jnp.zeros((wc, half), F32)
@@ -223,11 +218,12 @@
 
     near = order[1:]
     got_wy = {d: send(s["w_sum"].at[weight_rows(d)], s["wy"].at[d], at(dy=-d)) for d in near}
-    for copy in got_sg + got_qx:
-        copy.wait_recv()
-    value = lax.dot_general(sgx[...], qx[...], (((0,), (0,)), ((), ())), preferred_element_type=F32)
-    s["u_own"][...] = value[:yr]
-    s["u_sum"][...] = value.astype(BF16)
+    sgx = s["sgx"]
+    got_sg = [send(qx.at[pl.ds(0, q)], qx.at[pl.ds(d * q, q)], at(dx=d)) for d in range(1, nx)]
+    got_sg += [
+        send(s["sg"].at[d], sgx.at[pl.ds((nx - d) * q, q)], at(dx=-d)) for d in range(1, nx)
+    ]
+    sgx[pl.ds(0, q), :] = s["sg"][0]
     value = s["w_own"][weight_rows(0), :]
     for d in near:
         got_wy[d].wait_recv()
@@ -242,6 +238,11 @@
         send(s["wyb"].at[weight_block(dh)], wz.at[dh * nl + l], at(dh=-dh, dl=-dl))
         for dh, dl in along
     ]
+    for copy in got_sg:
+        copy.wait_recv()
+    value = lax.dot_general(sgx[...], qx[...], (((0,), (0,)), ((), ())), preferred_element_type=F32)
+    s["u_own"][...] = value[:yr]
+    s["u_sum"][...] = value.astype(BF16)
     got_uy = {
         d: send(s["u_sum"].at[pl.ds(d * yr, yr)], s["uy"].at[d], at(dy=-d)) for d in near
     }

time: 90.9 us -> 86.6 us (0.953)
  Pallas kernels: 86.4 us -> 82.7 us
    pallas_call x1, Pallas kernels: 86.4 us -> 82.7 us  [step(): pl.pallas_call(body, out_shape=(jax.ShapeDtypeStruct((ipd, emb), F32), ja...]
where the time goes in v3:
time: 86.6 us; the launch traced here: 86 us
  Pallas kernels  82.7 us (95%)
  local copies, waits for them, and re-layouts  2.7 us (3%)
    pallas_call x1, Pallas kernels, step(): pl.pallas_call(body, out_shape=(jax.ShapeDtypeStruct((ipd, emb), F32), ja...  82.7 us
    unnamed x2, local copies, waits for them, and re-layouts  2.7 us

profile of v3, /device:TPU:1, one launch (start us, length us, event | category | flops | bytes accessed | tf_op | source)
XLA Modules:
  0.0 86.0 jit_solution(6975405464349121921)
XLA Ops:
  0.6 82.7 %shard_map.68 = (f32[8,512]{1,0:T(8,128)}, f32[16,512]{1,0:T(8,128)}) custom-call(bf16[128,2048]{1,0:T(8,128)(2,1)} %refs_0_.1, bf16[2048,512]{1,0:T(8,128)(2,1)} %refs_1_.1, bf16[8,512]{1,0:T(8,128)(2,1)} %refs_2_.1, s32[1,128]{1,0:T(1,128)} %bitcast.3, s32[8,128]{1,0:T(8,128)} %bitcast.2), custom_call_target="tpu_custom_call" | custom-call | tf_op jit(solution)/shard_map/pallas_call | solution.py:344
  83.3 1.3 %copy.9 = f32[8,512]{1,0:T(8,128)} copy(f32[8,512]{1,0:T(8,128)} %get-tuple-element.4) | data formatting | bytes 32768
  84.6 1.4 %copy.10 = f32[16,512]{1,0:T(8,128)} copy(f32[16,512]{1,0:T(8,128)} %get-tuple-element.5) | data formatting | bytes 65536

commit v4 on v3

--- a/solution.py
+++ b/solution.py
@@ -11,6 +11,7 @@
 F32, BF16 = jnp.float32, jnp.bfloat16
 INV_TAU = 50.0
 EPSILON = 1e-06
+SIDE_AT = 3
 
 NX, NY, NH, NL, NC = 4, 8, 4, 3, 2
 
@@ -114,34 +115,37 @@
         return g.at[slot, pl.ds(d * yr, yr)]
 
     got_y = {d: send(piece(0, 0), piece(0, d), at(dy=d)) for d in range(1, ny)}
-    from_left, from_right, from_far = {}, {}, {}
-
     order = sorted(range(ny), key=lambda d: (min(d, ny - d), d))
-    relayed, lag = max(ny // 2, 1), 4
-
-    def pass_on(i):
-        d = order[i]
-        from_left[d].wait_recv()
-        if i < relayed and i % 2 == 0:
-            from_far[d] = send(piece(1, d), piece(2, d), right)
-        from_right[d].wait_recv()
-        if i < relayed and i % 2 == 1:
-            from_far[d] = send(piece(3, d), piece(2, d), left)
-
+    side = emb // 4
+    main, aside = pl.ds(0, emb - side), pl.ds(emb - side, side)
+    got_x = {1: [], 3: [], 2: []}
     for i, d in enumerate(order):
         if d:
             got_y[d].wait_recv()
-        from_left[d] = send(piece(0, d), piece(1, d), right)
-        from_right[d] = send(piece(0, d), piece(3, d), left)
-        if i >= relayed:
-            from_far[d] = send(piece(0, d), piece(2, d), far)
+        for slot, device in ((1, right), (3, left), (2, far)):
+            if d:
+                rows = pl.ds(d * yr, yr)
+                copy = send(g.at[0, rows, main], g.at[slot, rows, main], device)
+            else:
+                copy = send(piece(0, 0), piece(slot, 0), device)
+            got_x[slot].append(copy)
+        if i == min(SIDE_AT, ny - 1):
+            for slot in got_x:
+                got_x[slot].pop(0).wait_recv()
+            far_slots = pl.ds(1, nx - 1)
+            got_side = [
+                send(
+                    g.at[far_slots, pl.ds(0, yr), aside],
+                    g.at[far_slots, pl.ds(k * yr, yr), aside],
+                    at(dy=k),
+                )
+                for k in order[1:]
+            ]
         if i == min(2, ny - 1):
             for copy in got_hx:
                 copy.wait_recv()
             load_own.wait()
             got_hid = send(s["hx"].at[:, pl.ds(0, q)], s["hx"].at[:, pl.ds(q, q)], twin)
-        if i >= lag:
-            pass_on(i - lag)
 
     def column(ids):
         i, p = ids % ipd, ids // ipd
@@ -162,11 +166,11 @@
     picks = [jnp.zeros((q, 1), F32) for _ in ids]
     for slot in (0, 1, 3, 2):
         if slot == 1:
-            for i in range(max(ny - lag, 0), ny):
-                pass_on(i)
-        if slot == 2:
-            for d in range(ny):
-                from_far[d].wait_recv()
+            for copy in got_side:
+                copy.wait_recv()
+        if slot:
+            for copy in got_x[slot]:
+                copy.wait_recv()
         scores = lax.dot_general(
             qx[pl.ds(0, q), :], g[slot], (((1,), (1,)), ((), ())), preferred_element_type=F32
         )

time: 86.6 us -> 85.7 us (0.990)
  Pallas kernels: 82.7 us -> 81.2 us
    pallas_call x1, Pallas kernels: 82.7 us -> 81.2 us  [step(): pl.pallas_call(body, out_shape=(jax.ShapeDtypeStruct((ipd, emb), F32), ja...]
where the time goes in v4:
time: 85.7 us; the launch traced here: 84.6 us
  Pallas kernels  81.2 us (95%)
  local copies, waits for them, and re-layouts  2.7 us (3%)
    pallas_call x1, Pallas kernels, step(): pl.pallas_call(body, out_shape=(jax.ShapeDtypeStruct((ipd, emb), F32), ja...  81.2 us
    unnamed x2, local copies, waits for them, and re-layouts  2.7 us

profile of v4, /device:TPU:1, one launch (start us, length us, event | category | flops | bytes accessed | tf_op | source)
XLA Modules:
  0.0 84.6 jit_solution(12318948959706044696)
XLA Ops:
  0.6 81.2 %shard_map.68 = (f32[8,512]{1,0:T(8,128)}, f32[16,512]{1,0:T(8,128)}) custom-call(bf16[128,2048]{1,0:T(8,128)(2,1)} %refs_0_.1, bf16[2048,512]{1,0:T(8,128)(2,1)} %refs_1_.1, bf16[8,512]{1,0:T(8,128)(2,1)} %refs_2_.1, s32[1,128]{1,0:T(1,128)} %bitcast.3, s32[8,128]{1,0:T(8,128)} %bitcast.2), custom_call_target="tpu_custom_call" | custom-call | tf_op jit(solution)/shard_map/pallas_call | solution.py:348
  81.9 1.3 %copy.9 = f32[8,512]{1,0:T(8,128)} copy(f32[8,512]{1,0:T(8,128)} %get-tuple-element.4) | data formatting | bytes 32768
  83.2 1.4 %copy.10 = f32[16,512]{1,0:T(8,128)} copy(f32[16,512]{1,0:T(8,128)} %get-tuple-element.5) | data formatting | bytes 65536

commit v5 on v4

--- a/solution.py
+++ b/solution.py
@@ -11,7 +11,7 @@
 F32, BF16 = jnp.float32, jnp.bfloat16
 INV_TAU = 50.0
 EPSILON = 1e-06
-SIDE_AT = 3
+SIDE_AT = 1
 
 NX, NY, NH, NL, NC = 4, 8, 4, 3, 2
 

time: 85.7 us -> 84.5 us (0.986)
  Pallas kernels: 81.2 us -> 80.3 us
    pallas_call x1, Pallas kernels: 81.2 us -> 80.3 us  [step(): pl.pallas_call(body, out_shape=(jax.ShapeDtypeStruct((ipd, emb), F32), ja...]
where the time goes in v5:
time: 84.5 us; the launch traced here: 83.7 us
  Pallas kernels  80.3 us (95%)
  local copies, waits for them, and re-layouts  2.7 us (3%)
    pallas_call x1, Pallas kernels, step(): pl.pallas_call(body, out_shape=(jax.ShapeDtypeStruct((ipd, emb), F32), ja...  80.3 us
    unnamed x2, local copies, waits for them, and re-layouts  2.7 us

profile of v5, /device:TPU:1, one launch (start us, length us, event | category | flops | bytes accessed | tf_op | source)
XLA Modules:
  0.0 83.7 jit_solution(13782367686789207504)
XLA Ops:
  0.6 80.3 %shard_map.68 = (f32[8,512]{1,0:T(8,128)}, f32[16,512]{1,0:T(8,128)}) custom-call(bf16[128,2048]{1,0:T(8,128)(2,1)} %refs_0_.1, bf16[2048,512]{1,0:T(8,128)(2,1)} %refs_1_.1, bf16[8,512]{1,0:T(8,128)(2,1)} %refs_2_.1, s32[1,128]{1,0:T(1,128)} %bitcast.3, s32[8,128]{1,0:T(8,128)} %bitcast.2), custom_call_target="tpu_custom_call" | custom-call | tf_op jit(solution)/shard_map/pallas_call | solution.py:348
  81.0 1.3 %copy.9 = f32[8,512]{1,0:T(8,128)} copy(f32[8,512]{1,0:T(8,128)} %get-tuple-element.4) | data formatting | bytes 32768
  82.3 1.4 %copy.10 = f32[16,512]{1,0:T(8,128)} copy(f32[16,512]{1,0:T(8,128)} %get-tuple-element.5) | data formatting | bytes 65536

commit v6 on v5

--- a/solution.py
+++ b/solution.py
@@ -256,8 +256,7 @@
     value = functools.reduce(jnp.add, [wz[i].astype(F32) for i in range(nh * nl)])
     lc = s["lc"]
     lc[c] = value
-    send(lc.at[c], lc.at[c], twin).wait_recv()
-    weight_sum = jnp.concatenate([lc[0], lc[1]], axis=1)
+    got_lc = send(lc.at[c], lc.at[c], twin)
 
     def spread(name, value, devices):
         buffer = s[name]
@@ -269,14 +268,18 @@
             copy.wait_recv()
         return functools.reduce(jnp.add, [s[name][i] for i in range(len(copies) + 1)])
 
-    square = jnp.broadcast_to(jnp.sum(weight_sum * weight_sum, keepdims=True), (8, 128))
-    got_sq = spread("sqy", square, [at(dy=d) for d in range(1, ny)])
+    sqy = s["sqy"]
+    sqy[c] = jnp.broadcast_to(jnp.sum(value * value, keepdims=True), (8, 128))
+    places = [(dy, dc) for dy in range(ny) for dc in range(nc) if (dy, dc) != (0, 0)]
+    got_sq = [send(sqy.at[c], sqy.at[dy * nc + c], at(dy=dy, dc=dc)) for dy, dc in places]
     value = s["u_own"][...]
     for d in near:
         got_uy[d].wait_recv()
         value = value + s["uy"][d].astype(F32)
     s["uyf"][...] = value
     square = gather("sqy", got_sq)
+    got_lc.wait_recv()
+    weight_sum = jnp.concatenate([lc[0], lc[1]], axis=1)
     got_sq = spread("sqxh", square, [at(dx=dx, dh=dh) for dx, dh in across])
     got_uh = [
         send(s["uyf"].at[pl.ds(d * ipd, ipd)], s["uh"].at[d], at(dh=-d)) for d in range(1, nh)
@@ -332,7 +335,7 @@
         "uy": pltpu.VMEM((ny, yr, emb), BF16),
         "uyf": pltpu.VMEM((yr, emb), F32),
         "uh": pltpu.VMEM((nh, ipd, emb), F32),
-        "sqy": pltpu.VMEM((ny, 8, 128), F32),
+        "sqy": pltpu.VMEM((ny * nc, 8, 128), F32),
         "sqxh": pltpu.VMEM((nx * nh, 8, 128), F32),
         "send": pltpu.SemaphoreType.DMA((copies,)),
         "recv": pltpu.SemaphoreType.DMA((copies,)),

time: 84.5 us -> 84.1 us (level)
  no operation moved by 1% of the time
where the time goes in v6:
time: 84.1 us; the launch traced here: 83.8 us
  Pallas kernels  80.5 us (96%)
  local copies, waits for them, and re-layouts  2.7 us (3%)
    pallas_call x1, Pallas kernels, step(): pl.pallas_call(body, out_shape=(jax.ShapeDtypeStruct((ipd, emb), F32), ja...  80.5 us
    unnamed x2, local copies, waits for them, and re-layouts  2.7 us

profile of v6, /device:TPU:1, one launch (start us, length us, event | category | flops | bytes accessed | tf_op | source)
XLA Modules:
  0.0 83.8 jit_solution(4876999819016623695)
XLA Ops:
  0.6 80.5 %shard_map.68 = (f32[8,512]{1,0:T(8,128)}, f32[16,512]{1,0:T(8,128)}) custom-call(bf16[128,2048]{1,0:T(8,128)(2,1)} %refs_0_.1, bf16[2048,512]{1,0:T(8,128)(2,1)} %refs_1_.1, bf16[8,512]{1,0:T(8,128)(2,1)} %refs_2_.1, s32[1,128]{1,0:T(1,128)} %bitcast.3, s32[8,128]{1,0:T(8,128)} %bitcast.2), custom_call_target="tpu_custom_call" | custom-call | tf_op jit(solution)/shard_map/pallas_call | solution.py:351
  81.1 1.3 %copy.9 = f32[8,512]{1,0:T(8,128)} copy(f32[8,512]{1,0:T(8,128)} %get-tuple-element.4) | data formatting | bytes 32768
  82.5 1.4 %copy.10 = f32[16,512]{1,0:T(8,128)} copy(f32[16,512]{1,0:T(8,128)} %get-tuple-element.5) | data formatting | bytes 65536
